TPU v7x, 32 devices: a whole 2x2x4 slice. The times are simulated.
32 devices in a mesh: shard: 8 (over z, y), rep: 4 (over x, core).
Axes of the slice: x: 2, y: 2, z: 4, core: 2. Of those that a mesh axis runs over, the one named last changes fastest.
Arguments:
- node_feat: bfloat16 [256, 128, 256], P(('shard', 'rep'))
- node_cot: bfloat16 [256, 128, 256], P(('shard', 'rep'))
- edge_length: float32 [256, 1536], P(('shard', 'rep')), may hold values from 0.5 to 5.5
- atom_count: int32 [256], P(('shard', 'rep')), may hold values from 32 to 128, as said below
- edge_count: int32 [256], P(('shard', 'rep')), may hold values from 384 to 1536, as said below
- edge_source: int32 [256, 1536], P(('shard', 'rep')), may hold values from 0 to 127, as said below
- edge_target: int32 [256, 1536], P(('shard', 'rep')), may hold values from 0 to 127, as said below
- dataset_tag: int32 [256], P(('shard', 'rep')), may hold values from 0 to 1
- charge_tag: int32 [256], P(('shard', 'rep')), may hold values from 0 to 1
- spin_tag: int32 [256], P(('shard', 'rep')), may hold values from 0 to 1
- dataset_gain: float32 [2, 32], replicated, may hold values from 0.2 to 5
- charge_gain: float32 [2, 32], replicated, may hold values from 0.2 to 5
- spin_gain: float32 [2, 32], replicated, may hold values from 0.2 to 5
- params: float32 [32, 128, 2, 128], P(None, 'shard'), may hold values from -0.375 to 0.375
- moment_one: float32 [32, 128, 2, 128], P(None, 'shard'), may hold values from -0.9 to 0.9
- moment_two: float32 [32, 128, 2, 128], P(None, 'shard'), may hold values from 0.0001 to 0.01
Outputs:
- new_params: float32 [32, 128, 2, 128], P(None, 'shard')
- new_moment_one: float32 [32, 128, 2, 128], P(None, 'shard')
- new_moment_two: float32 [32, 128, 2, 128], P(None, 'shard')
- full_weights: bfloat16 [32, 128, 2, 128], replicated
Inputs may be any that keep to these rules, and one draw needn't show every extreme that they name: `atom_count`: every system has at least a quarter of its atom slots filled. `edge_count`: every system has at least a quarter of its edge slots live. `edge_source`: every slot, live or not, names an atom below its system's atom count. `edge_target`: every slot, live or not, names an atom below its system's atom count.
All inputs are finite; a program needn't handle non-finite values.
Results may differ from a plain program's by a relative error of at most 0.0036.
Values may be sent and summed in bfloat16 or wider, within the bound.
A program may use at most 64 MiB of HBM per device.

v0:
```python
import math

import jax
import jax.numpy as jnp
from jax import lax
from jax.sharding import PartitionSpec as P

STEP = 10


beta_one = 0.9
beta_two = 0.999
adam_eps = 1e-08
learn_rate = 0.01
decay_rate = 0.01
cutoff_radius = 6.0


def envelope(length):
    ratio = length / cutoff_radius
    return 1.0 - 21.0 * ratio**5 + 35.0 * ratio**6 - 15.0 * ratio**7


def mixing_table(dataset_gain, charge_gain, spin_gain):
    product_table = (
        dataset_gain[:, None, None, :] * charge_gain[None, :, None, :] * spin_gain[None, None, :, :]
    )
    product_table = product_table.reshape(-1, product_table.shape[-1])
    return product_table / jnp.sum(product_table, axis=1, keepdims=True)


def onehot_rows(dataset_tag, charge_tag, spin_tag, charge_count, spin_count, row_total):
    tag_rows = (dataset_tag * charge_count + charge_tag) * spin_count + spin_tag
    return (tag_rows[:, None] == jnp.arange(row_total, dtype=jnp.int32)[None, :]).astype(
        jnp.float32
    )


def select_rows(node_rows, slot_ids):
    atom_ids = lax.broadcasted_iota(jnp.int32, (1, node_rows.shape[0]), 1)
    selector = (slot_ids[:, None] == atom_ids).astype(jnp.bfloat16)
    return jnp.dot(selector, node_rows, preferred_element_type=jnp.float32)


def system_product(items):
    feat_rows, cot_rows, length_row, atoms_here, edges_here, source_row, target_row = items
    atom_slots = feat_rows.shape[0]
    edge_input = (select_rows(feat_rows, source_row) * envelope(length_row)[:, None]).astype(
        jnp.bfloat16
    )
    slot_index = lax.broadcasted_iota(jnp.int32, source_row.shape, 0)
    live_mask = (slot_index < edges_here).astype(jnp.float32)
    factor = live_mask * (float(atom_slots) / atoms_here.astype(jnp.float32))
    edge_grad = (select_rows(cot_rows, target_row) * factor[:, None]).astype(jnp.bfloat16)
    return lax.dot_general(
        edge_input, edge_grad, (((0,), (0,)), ((), ())), preferred_element_type=jnp.float32
    )


def adam_update(gradients, params, moment_one, moment_two, square_sum, norm_limit):
    clip_factor = jnp.minimum(1.0, norm_limit / (jnp.sqrt(square_sum) + 1e-06))
    clipped = clip_factor * gradients
    new_one = beta_one * moment_one + (1.0 - beta_one) * clipped
    new_two = beta_two * moment_two + (1.0 - beta_two) * clipped * clipped
    first_fix = 1.0 - beta_one**STEP
    second_fix = 1.0 - beta_two**STEP
    direction = new_one / first_fix / (jnp.sqrt(new_two / second_fix) + adam_eps)
    new_params = params - learn_rate * (direction + decay_rate * params)
    return (new_params, new_one, new_two)


def local(
    node_feat,
    node_cot,
    edge_length,
    atom_count,
    edge_count,
    edge_source,
    edge_target,
    dataset_tag,
    charge_tag,
    spin_tag,
    dataset_gain,
    charge_gain,
    spin_gain,
    params,
    moment_one,
    moment_two,
):
    channels = node_feat.shape[2] // 2
    mixing = mixing_table(dataset_gain, charge_gain, spin_gain)
    tag_onehot = onehot_rows(
        dataset_tag, charge_tag, spin_tag, charge_gain.shape[0], spin_gain.shape[0], mixing.shape[0]
    )
    products = lax.map(
        system_product,
        (node_feat, node_cot, edge_length, atom_count, edge_count, edge_source, edge_target),
    )
    real_part = products[:, :channels, :channels] + products[:, channels:, channels:]
    imag_part = products[:, :channels, channels:] - products[:, channels:, :channels]
    system_grad = jnp.stack([real_part, imag_part], axis=2)
    local_term = jnp.einsum(
        "sk,scto->ckto", tag_onehot, system_grad, precision=lax.Precision.HIGHEST
    )
    summed = lax.psum_scatter(local_term, "shard", scatter_dimension=0, tiled=True)
    summed = lax.psum(summed, "rep")
    gradients = jnp.einsum("ke,ckto->ecto", mixing, summed, precision=lax.Precision.HIGHEST)
    square_sum = lax.psum(jnp.sum(gradients * gradients), "shard")
    norm_limit = math.sqrt(mixing.shape[1] * 2 * channels * channels)
    new_params, new_one, new_two = adam_update(
        gradients, params, moment_one, moment_two, square_sum, norm_limit
    )
    full_weights = lax.all_gather(new_params.astype(jnp.bfloat16), "shard", axis=1, tiled=True)
    return (new_params, new_one, new_two, full_weights)


def solution(mesh):
    placed = (
        P(("shard", "rep"), None, None),
        P(("shard", "rep"), None, None),
        P(("shard", "rep"), None),
        P(("shard", "rep")),
        P(("shard", "rep")),
        P(("shard", "rep"), None),
        P(("shard", "rep"), None),
        P(("shard", "rep")),
        P(("shard", "rep")),
        P(("shard", "rep")),
        P(),
        P(),
        P(),
        P(None, "shard", None, None),
        P(None, "shard", None, None),
        P(None, "shard", None, None),
    )
    return jax.shard_map(
        local,
        mesh=mesh,
        in_specs=placed,
        out_specs=(
            P(None, "shard", None, None),
            P(None, "shard", None, None),
            P(None, "shard", None, None),
            P(),
        ),
        check_vma=False,
    )
```

profile of v0, /device:TPU:1, one launch (start us, length us, event | category | flops | bytes accessed | tf_op | source)
XLA Modules:
  0.0 269.5 jit_solution(18076666228939215978)
XLA Ops:
  7.2 75.9 %while.10 = (s32[]{:T(128)}, f32[8,256,256]{2,1,0:T(8,128)S(1)}, s32[8,1536]{1,0:T(8,128)}, bf16[8,128,256]{2,1,0:T(8,128)(2,1)}, f32[8,1536]{1,0:T(8,128)}, /*i...) while((s32[]{:T(128)}, f32[8,256,256]{2,1,0:T(8,128)S(1)}, ...), condition=%wide.region_2.3_spmd, body=%wide.region_1.2_spmd.sunk | while | flops 404642304 | bytes 2051253 | solution.py:95
  7.2 1.2 dynamic_slice.48
  8.5 1.2 dynamic_slice.47
  12.8 2.2 fusion.52
  15.0 1.7 fusion.54
  16.7 1.2 dynamic_slice.48
  18.0 1.2 dynamic_slice.47
  21.4 0.9 dynamic-slice_reduce_fusion.3
  22.3 2.2 fusion.52
  24.5 1.7 fusion.54
  26.2 1.2 dynamic_slice.48
  27.4 1.2 dynamic_slice.47
  30.9 0.9 dynamic-slice_reduce_fusion.3
  31.8 2.2 fusion.52
  34.0 1.7 fusion.54
  35.7 1.2 dynamic_slice.48
  36.9 1.2 dynamic_slice.47
  40.4 0.9 dynamic-slice_reduce_fusion.3
  41.2 2.2 fusion.52
  43.4 1.7 fusion.54
  45.2 1.2 dynamic_slice.48
  46.4 1.2 dynamic_slice.47
  49.9 0.9 dynamic-slice_reduce_fusion.3
  50.7 2.2 fusion.52
  52.9 1.7 fusion.54
  54.7 1.2 dynamic_slice.48
  55.9 1.2 dynamic_slice.47
  60.2 2.2 fusion.52
  62.4 1.7 fusion.54
  64.2 1.2 dynamic_slice.48
  65.4 1.2 dynamic_slice.47
  69.7 2.2 fusion.52
  71.9 1.7 fusion.54
  73.6 1.2 dynamic_slice.48
  74.9 1.2 dynamic_slice.47
  79.2 2.2 fusion.52
  81.4 1.7 fusion.54
  83.9 2.2 convolution_bitcast_fusion
  86.2 64.7 %reduce-scatter.2.cloned.1.call-done = f32[16,8,2,128]{3,1,2,0:T(8,128)} async-done(((f32[128,8,2,128]{3,1,2,0:T(8,128)}), f32[16,8,2,128]{3,1,2,0:T(8,128)}) %reduce-scatter.2.cloned.1.call-update) | async-done | bytes 131088 | tf_op jit(solution)/shard_map/reduce_scatter | solution.py:105
  151.1 32.8 %all-reduce.2.cloned.1.call-done = f32[16,8,2,128]{3,1,2,0:T(8,128)} async-done(((f32[16,8,2,128]{3,1,2,0:T(8,128)}), f32[16,8,2,128]{3,1,2,0:T(8,128)}) %all-reduce.2.cloned.1.call-update) | async-done | bytes 131088 | tf_op jit(solution)/shard_map/psum | solution.py:106
  183.9 2.3 multiply_reduce_fusion.1
  186.2 18.6 %psum.15 = f32[]{:T(128)} all-reduce(f32[]{:T(128)} %get-tuple-element.88), channel_id=1, replica_groups=mesh['shard'=8,'rep'=4] {'shard'}, use_global_device_ids=true, to_apply=%region_6.7 | all-reduce | flops 1 | bytes 8 | tf_op jit(solution)/shard_map/psum | solution.py:108
  205.5 2.9 %fusion.36 = (bf16[32,16,2,128]{3,0,2,1:T(8,128)(2,1)}, f32[32,16,2,128]{3,0,2,1:T(8,128)S(1)}, f32[32,16,2,128]{3,0,2,1:T(8,128)S(1)}, f32[32,16,2,128]{3,0,2,1:T(8,128)S(1)}) fusion(f32[32,16,2,128]{3,2,1,0:T(2,128)S(1)} %copy-done, f32[32,16,2,128]{3,0,2,1:T(8,128)S(1)} %get-tuple-element.89, f32[]{:T(128)S(6)} %min.3, ...), kind=kLoop, calls=%fused_computation.56 | loop fusion | flops 2228224 | bytes 3932164 | tf_op jit(solution)/shard_map/convert_element_type | solution.py:113
  208.5 1.2 copy.32
  209.7 1.2 copy.33
  210.9 1.2 copy.34
  212.1 45.8 %all-gather.2.cloned.1.call-done = bf16[32,128,2,128]{3,0,2,1:T(8,128)(2,1)} async-done(((bf16[32,16,2,128]{3,0,2,1:T(8,128)(2,1)}), bf16[32,128,2,128]{3,0,2,1:T(8,128)(2,1)}) %all-gather.2.cloned.1.call-update) | async-done | bytes 2097168 | tf_op jit(solution)/shard_map/all_gather | solution.py:113
  257.9 5.1 %copy.35 = bf16[32,128,2,128]{3,2,1,0:T(2,128)(2,1)} copy(bf16[32,128,2,128]{3,0,2,1:T(8,128)(2,1)} %all-gather.2.cloned.1.call-done) | data formatting | bytes 4194304
  (57 shorter events, 16.4 us)
Async XLA Ops:
  7.2 143.7 %reduce-scatter.2.cloned.1.call-start = ((), (), s32[]{:S(2)}) async-start(), calls=%async_computation.1 | async-start | bytes 1179648 | tf_op jit(solution)/shard_map/reduce_scatter | solution.py:105
  83.1 0.7 copy-start.5
  83.1 0.7 copy-start.6
  83.2 0.7 copy-start.7
  83.8 2.3 copy-start.3
  83.8 2.3 copy-start.4
  83.8 67.1 %copy-start.2 = (f32[2,32]{1,0:T(2,128)S(1)}, f32[2,32]{1,0:T(2,128)}, u32[]{:S(2)}) copy-start(f32[2,32]{1,0:T(2,128)} %param.30) | copy-start | bytes 772
  83.8 121.7 %copy-start = (f32[32,16,2,128]{3,2,1,0:T(2,128)S(1)}, f32[32,16,2,128]{3,2,1,0:T(2,128)}, u32[]{:S(2)}) copy-start(f32[32,16,2,128]{3,2,1,0:T(2,128)} %param.31) | copy-start | bytes 1572868
  83.8 121.7 %copy-start.1 = (f32[32,16,2,128]{3,2,1,0:T(2,128)S(1)}, f32[32,16,2,128]{3,2,1,0:T(2,128)}, u32[]{:S(2)}) copy-start(f32[32,16,2,128]{3,2,1,0:T(2,128)} %param.32) | copy-start | bytes 1572868
  86.1 97.8 %all-reduce.2.cloned.1.call-start = ((), (), s32[]{:S(2)}) async-start(), calls=%async_computation.2 | async-start | bytes 262144 | tf_op jit(solution)/shard_map/psum | solution.py:106
  150.9 107.0 %all-gather.2.cloned.1.call-start = ((), (), s32[]{:S(2)}) async-start(), calls=%async_computation.3 | async-start | bytes 2359296 | tf_op jit(solution)/shard_map/all_gather | solution.py:113
Sparse Core Ops, SparseCore 0:
  86.2 64.6 reduce-scatter.1
  153.3 30.5 all-reduce.1
  208.6 49.2 all-gather.1
where the time goes:
time: 273 us; the launch traced here: 270 us
  waiting for transfers between devices  143 us (52%)
  local copies, waits for them, and re-layouts  36.1 us (13%)
  matrix products  35.8 us (13%)
  blocking collectives  18.6 us (7%)
  other arithmetic  15.1 us (6%)
  between operations  14.6 us (5%)
  loops' own time  5.91 us (2%)
    reduce_scatter x1, waiting for transfers between devices, local(): lax.psum_scatter(local_term, 'shard', scatter_dimension=0, tiled=True)  64.7 us
    all_gather x1, waiting for transfers between devices, local(): lax.all_gather(new_params.astype(jnp.bfloat16), 'shard', axis=1, tiled=True)  45.8 us
    psum x1, waiting for transfers between devices, local(): summed = lax.psum(summed, 'rep')  32.8 us
    dynamic_slice x24, local copies, waits for them, and re-layouts, local(): lax.map(system_product, (node_feat, node_cot, edge_length, atom_count, ed...  26.8 us
    psum x1, blocking collectives, local(): square_sum = lax.psum(jnp.sum(gradients * gradients), 'shard')  18.6 us
    dot_general x8, matrix products, select_rows(): return jnp.dot(selector, node_rows, preferred_element_type=jnp.float32)  17.5 us
    dot_general x8, matrix products, system_product(): lax.dot_general(edge_input, edge_grad, (((0,), (0,)), ((), ())), preferre...  13.8 us
    unnamed x20, local copies, waits for them, and re-layouts  9.22 us
  transfers between devices with their start and end apart: 3, of which 3 were waited for; matrix products, arithmetic and copies ran while one was open for 1% of the time, Pallas kernels for 0%

commit v1 on v0

--- a/solution.py
+++ b/solution.py
@@ -1,8 +1,11 @@
+import functools
 import math
 
 import jax
 import jax.numpy as jnp
 from jax import lax
+from jax.experimental import pallas as pl
+from jax.experimental.pallas import tpu as pltpu
 from jax.sharding import PartitionSpec as P
 
 STEP = 10
@@ -69,7 +72,7 @@
     return (new_params, new_one, new_two)
 
 
-def local(
+def plain_local(
     node_feat,
     node_cot,
     edge_length,
@@ -114,6 +117,369 @@
     return (new_params, new_one, new_two, full_weights)
 
 
+MIB = 1024 * 1024
+MESH = pl.DeviceIdType.MESH
+
+
+def split_dot(left, right, contract):
+    high = right.astype(jnp.bfloat16)
+    low = (right - high.astype(jnp.float32)).astype(jnp.bfloat16)
+    dims = (contract, ((), ()))
+    return lax.dot_general(
+        left, high, dims, preferred_element_type=jnp.float32
+    ) + lax.dot_general(left, low, dims, preferred_element_type=jnp.float32)
+
+
+def partial_kernel(
+    charge_count, spin_count, reps, feat, cot, length, atoms, edges, source, target,
+    dataset, charge, spin, pieces, grouped,
+):
+    systems, slots, width = feat.shape
+    channels = width // 2
+    lanes = source.shape[1]
+    grouped[...] = jnp.zeros_like(grouped)
+    weight = envelope(length[...])
+    slot_index = lax.broadcasted_iota(jnp.int32, (1, lanes), 1)
+    atom_index = lax.broadcasted_iota(jnp.int32, (slots, lanes), 0)
+    for s in range(systems):
+        count = jnp.full((1, lanes), atoms[s], jnp.int32).astype(jnp.float32)
+        factor = jnp.where(slot_index < edges[s], float(slots) / count, 0.0)
+        row = weight[s : s + 1, :] * factor
+        left = jnp.where(atom_index == source[s : s + 1, :], row, 0.0).astype(jnp.bfloat16)
+        right = jnp.where(atom_index == target[s : s + 1, :], 1.0, 0.0).astype(jnp.bfloat16)
+        pairs = lax.dot_general(
+            right, left, (((1,), (1,)), ((), ())), preferred_element_type=jnp.float32
+        )
+        mixed = split_dot_left(pairs, cot[s])
+        real, imag = mixed[:, :channels], mixed[:, channels:]
+        block = jnp.concatenate(
+            [
+                jnp.concatenate([real, imag], axis=1),
+                jnp.concatenate([imag, -real], axis=1),
+            ],
+            axis=0,
+        )
+        rows = feat[s]
+        stacked = jnp.concatenate([rows[:, :channels], rows[:, channels:]], axis=0)
+        product = split_dot(stacked, block, ((0,), (0,)))
+        tag = (dataset[s] * charge_count + charge[s]) * spin_count + spin[s]
+        grouped[tag, pl.ds(0, channels, stride=2), :] += product[:, :channels]
+        grouped[tag, pl.ds(1, channels, stride=2), :] += product[:, channels:]
+    tags = grouped.shape[0]
+    shards = pieces.shape[2]
+    for s in range(shards):
+        for r in range(reps):
+            at = (s * reps + r) * 8
+            pieces[r % 2, r // 2, s] = (
+                grouped[:, at : at + 8, :].reshape(tags * 8, channels).astype(jnp.bfloat16)
+            )
+
+
+def split_dot_left(left, right):
+    high = left.astype(jnp.bfloat16)
+    low = (left - high.astype(jnp.float32)).astype(jnp.bfloat16)
+    dims = (((0,), (0,)), ((), ()))
+    return lax.dot_general(
+        high, right, dims, preferred_element_type=jnp.float32
+    ) + lax.dot_general(low, right, dims, preferred_element_type=jnp.float32)
+
+
+def expert_rows(mixing, summed, expert):
+    total = mixing[0, expert] * summed[:, 0]
+    for k in range(1, summed.shape[1]):
+        total = total + mixing[k, expert] * summed[:, k]
+    return total
+
+
+def adam_rows(gradient, clip, params, moment_one, moment_two):
+    clipped = clip * gradient
+    new_one = beta_one * moment_one + (1.0 - beta_one) * clipped
+    new_two = beta_two * moment_two + (1.0 - beta_two) * clipped * clipped
+    first_fix = 1.0 - beta_one**STEP
+    second_fix = 1.0 - beta_two**STEP
+    direction = new_one / first_fix / (jnp.sqrt(new_two / second_fix) + adam_eps)
+    return params - learn_rate * (direction + decay_rate * params), new_one, new_two
+
+
+def exchange_kernel(
+    shards, reps, norm_limit, mixing, pieces, params, moment_one, moment_two,
+    summed, clip_out, weights, pair_in, pair_sum, slices, norms,
+    pair_sem, slice_send, slice_recv, rep_send, rep_recv, norm_send, norm_recv,
+    z_send, z_recv, y_send, y_recv, x_send, x_recv, core_send, core_recv,
+):
+    shard, rep = lax.axis_index("shard"), lax.axis_index("rep")
+    planes, columns, depth = reps // 2, 2, shards // 2
+    x, core = rep // 2, rep % 2
+    z, y = shard // 2, shard % 2
+    devices = shards * reps
+    me = shard * reps + rep
+    experts = params.shape[0]
+    tags = summed.shape[1]
+
+    barrier = pltpu.get_barrier_semaphore()
+    for j in range(1, devices):
+        other = lax.rem(me + j, devices)
+        pl.semaphore_signal(
+            barrier, inc=1, device_id=(other // reps, lax.rem(other, reps)), device_id_type=MESH
+        )
+    pl.semaphore_wait(barrier, devices - 1)
+
+    def send(src, dst, send_sem, recv_sem, to):
+        copy = pltpu.make_async_remote_copy(
+            src_ref=src, dst_ref=dst, send_sem=send_sem, recv_sem=recv_sem,
+            device_id=to, device_id_type=MESH,
+        )
+        copy.start()
+        return copy
+
+    sibling = (shard, x * 2 + 1 - core)
+    started = []
+
+    pair = [
+        send(pieces.at[1 - core, i], pair_in.at[i], pair_sem.at[0, i], pair_sem.at[1, i], sibling)
+        for i in range(planes)
+    ]
+    for i in range(planes):
+        pair[i].wait_recv()
+        pair_sum[i] = (
+            pieces[core, i].astype(jnp.float32) + pair_in[i].astype(jnp.float32)
+        ).astype(jnp.bfloat16)
+    started += pair
+
+    arriving = []
+    for ds in range(shards):
+        for dx in range(planes):
+            if ds == 0 and dx == 0:
+                continue
+            to_x, to_s = lax.rem(x + dx, planes), lax.rem(shard + ds, shards)
+            j = dx * shards + ds
+            arriving.append(
+                send(
+                    pair_sum.at[to_x, to_s], slices.at[j], slice_send.at[j], slice_recv.at[j],
+                    (to_s, to_x * 2 + core),
+                )
+            )
+    total = pair_sum[x, shard].astype(jnp.float32)
+    for copy in arriving:
+        copy.wait_recv()
+    for j in range(1, planes * shards):
+        total = total + slices[j].astype(jnp.float32)
+    started += arriving
+    own = total.reshape(tags, 8, total.shape[-1])
+    summed[rep] = own
+
+    shared = []
+    for j in range(1, reps):
+        shared.append(
+            send(
+                summed.at[rep], summed.at[rep], rep_send.at[j], rep_recv.at[j],
+                (shard, lax.rem(rep + j, reps)),
+            )
+        )
+    squares = jnp.zeros(own.shape[1:], jnp.float32)
+    for e in range(experts):
+        gradient = expert_rows(mixing, own[None], e)[0]
+        squares = squares + gradient * gradient
+    norms[me] = squares
+    normed = []
+    for j in range(1, devices):
+        other = lax.rem(me + j, devices)
+        normed.append(
+            send(
+                norms.at[me], norms.at[me], norm_send.at[j], norm_recv.at[j],
+                (other // reps, lax.rem(other, reps)),
+            )
+        )
+    for copy in shared:
+        copy.wait_recv()
+    for copy in normed:
+        copy.wait_recv()
+    started += shared + normed
+    square_sum = jnp.sum(jnp.sum(norms[...], axis=0), axis=(0, 1), keepdims=True)
+    clip = jnp.minimum(1.0, norm_limit / (jnp.sqrt(square_sum) + 1e-06))
+    clip_out[...] = jnp.broadcast_to(clip, clip_out.shape)
+
+    half = experts // 2
+    span = (half * 5) // 8
+    only = half - span
+    first = core * half + x * only
+    cross = core * half + x * (half - only)
+    cross_other = core * half + (1 - x) * (half - only)
+    rows = weights.shape[1] // shards
+
+    def update(i, carry):
+        e = lax.rem(first + i, experts)
+        new_params, _, _ = adam_rows(
+            expert_rows(mixing, summed, e), clip, params[e], moment_one[e], moment_two[e]
+        )
+        weights[e, pl.ds(pl.multiple_of(shard * rows, rows), rows), :] = new_params.reshape(
+            rows, new_params.shape[-1]
+        ).astype(jnp.bfloat16)
+        return carry
+
+    lax.fori_loop(0, span, update, 0)
+
+    def pass_on(begin, count, owner, send_sem, recv_sem, to):
+        block = weights.at[
+            pl.ds(begin, count), pl.ds(pl.multiple_of(owner * rows, rows), rows), :
+        ]
+        copy = send(block, block, send_sem, recv_sem, to)
+        started.append(copy)
+        return copy
+
+    beside = (z * 2 + 1 - y, rep)
+    across = (shard, (1 - x) * 2 + core)
+    along, turned = [None] * depth, [None] * depth
+    turned[0] = pass_on(first, span, shard, y_send.at[0], y_recv.at[0], beside)
+    for d in range(1, depth):
+        to = lax.rem(z + d, depth) * 2 + y
+        along[d] = pass_on(first, span, shard, z_send.at[d], z_recv.at[d], (to, rep))
+    lax.fori_loop(span, experts, update, 0)
+
+    crossed, paired = [], []
+
+    def arrived(slot, owner):
+        crossed.append(
+            (slot, owner, pass_on(cross, only, owner, x_send.at[slot], x_recv.at[slot], across))
+        )
+        paired.append(
+            pass_on(first, span, owner, core_send.at[slot], core_recv.at[slot], sibling)
+        )
+
+    for d in range(depth):
+        if d > 0:
+            along[d].wait_recv()
+            owner = lax.rem(z + depth - d, depth) * 2 + y
+            turned[d] = pass_on(first, span, owner, y_send.at[d], y_recv.at[d], beside)
+            arrived(d, owner)
+        turned[d].wait_recv()
+        arrived(depth + d, lax.rem(z + depth - d, depth) * 2 + 1 - y)
+    for slot, owner, copy in crossed:
+        copy.wait_recv()
+        at = shards + slot
+        paired.append(
+            pass_on(cross_other, only, owner, core_send.at[at], core_recv.at[at], sibling)
+        )
+    for copy in paired:
+        copy.wait_recv()
+    for copy in started:
+        copy.wait_send()
+
+
+def finish_kernel(
+    mixing, summed, clip, params, moment_one, moment_two, gathered,
+    new_params, new_one, new_two, weights, sem,
+):
+    step = pl.program_id(0)
+    copy = pltpu.make_async_copy(gathered, weights, sem)
+
+    @pl.when(step == 0)
+    def _():
+        copy.start()
+
+    block = params.shape[0]
+    factor = clip[0:1, 0:1]
+
+    def update(i, carry):
+        gradient = expert_rows(mixing, summed, step * block + i)
+        new_params[i], new_one[i], new_two[i] = adam_rows(
+            gradient, factor, params[i], moment_one[i], moment_two[i]
+        )
+        return carry
+
+    lax.fori_loop(0, block, update, 0, unroll=2)
+
+    @pl.when(step == pl.num_programs(0) - 1)
+    def _():
+        copy.wait()
+
+
+def kernel_local(shards, reps, *args):
+    (
+        node_feat, node_cot, edge_length, atom_count, edge_count, edge_source, edge_target,
+        dataset_tag, charge_tag, spin_tag, dataset_gain, charge_gain, spin_gain,
+        params, moment_one, moment_two,
+    ) = args
+    experts, own_channels, parts, channels = params.shape
+    mixing = mixing_table(dataset_gain, charge_gain, spin_gain)
+    tags = mixing.shape[0]
+    planes = reps // 2
+    f32, bf16 = jnp.float32, jnp.bfloat16
+    vmem = pl.BlockSpec(memory_space=pltpu.VMEM)
+    smem = pl.BlockSpec(memory_space=pltpu.SMEM)
+    dma = pltpu.SemaphoreType.DMA
+    slice_rows = tags * 8
+
+    pieces = pl.pallas_call(
+        functools.partial(partial_kernel, charge_gain.shape[0], spin_gain.shape[0], reps),
+        out_shape=jax.ShapeDtypeStruct((2, planes, shards, slice_rows, channels), bf16),
+        in_specs=[vmem, vmem, vmem, smem, smem, vmem, vmem, smem, smem, smem],
+        out_specs=vmem,
+        scratch_shapes=[pltpu.VMEM((tags, channels * parts, channels), f32)],
+        compiler_params=pltpu.CompilerParams(vmem_limit_bytes=24 * MIB),
+        name="partial_sums",
+    )(
+        node_feat, node_cot, edge_length, atom_count, edge_count, edge_source, edge_target,
+        dataset_tag, charge_tag, spin_tag,
+    )
+    rows = own_channels * parts
+    states = [a.reshape(experts, reps, 8, channels) for a in (params, moment_one, moment_two)]
+    norm_limit = math.sqrt(experts * parts * channels * channels)
+    depth = shards // 2
+    summed, clip, gathered = pl.pallas_call(
+        functools.partial(exchange_kernel, shards, reps, norm_limit),
+        out_shape=(
+            jax.ShapeDtypeStruct((reps, tags, 8, channels), f32),
+            jax.ShapeDtypeStruct((8, channels), f32),
+            jax.ShapeDtypeStruct((experts, shards * rows, channels), bf16),
+        ),
+        in_specs=[smem, vmem, vmem, vmem, vmem],
+        out_specs=(vmem, vmem, vmem),
+        scratch_shapes=[
+            pltpu.VMEM((planes, shards, slice_rows, channels), bf16),
+            pltpu.VMEM((planes, shards, slice_rows, channels), bf16),
+            pltpu.VMEM((planes * shards, slice_rows, channels), bf16),
+            pltpu.VMEM((shards * reps, 8, channels), f32),
+            dma((2, planes)),
+            dma((planes * shards,)),
+            dma((planes * shards,)),
+            dma((reps,)),
+            dma((reps,)),
+            dma((shards * reps,)),
+            dma((shards * reps,)),
+            dma((depth,)),
+            dma((depth,)),
+            dma((depth,)),
+            dma((depth,)),
+            dma((shards,)),
+            dma((shards,)),
+            dma((2 * shards,)),
+            dma((2 * shards,)),
+        ],
+        compiler_params=pltpu.CompilerParams(
+            collective_id=0, has_side_effects=True, vmem_limit_bytes=24 * MIB
+        ),
+        name="exchange",
+    )(mixing, pieces, *states)
+
+    steps = 4
+    block = pl.BlockSpec((experts // steps, reps, 8, channels), lambda i: (i, 0, 0, 0))
+    state = jax.ShapeDtypeStruct(states[0].shape, f32)
+    anywhere = pl.BlockSpec(memory_space=pl.ANY)
+    outs = pl.pallas_call(
+        finish_kernel,
+        grid=(steps,),
+        out_shape=(state, state, state, jax.ShapeDtypeStruct(gathered.shape, bf16)),
+        in_specs=[smem, vmem, vmem, block, block, block, anywhere],
+        out_specs=(block, block, block, anywhere),
+        scratch_shapes=[dma],
+        compiler_params=pltpu.CompilerParams(vmem_limit_bytes=16 * MIB),
+        name="finish",
+    )(mixing, summed, clip, *states, gathered)
+    local_states = [a.reshape(params.shape) for a in outs[:3]]
+    return (*local_states, outs[3].reshape(experts, shards * own_channels, parts, channels))
+
+
 def solution(mesh):
     placed = (
         P(("shard", "rep"), None, None),
@@ -133,6 +499,14 @@
         P(None, "shard", None, None),
         P(None, "shard", None, None),
     )
+    shards, reps = mesh.shape["shard"], mesh.shape["rep"]
+
+    def local(*args):
+        params = args[13]
+        if reps == 4 and shards % 2 == 0 and params.shape[1] * params.shape[2] == 8 * reps:
+            return kernel_local(shards, reps, *args)
+        return plain_local(*args)
+
     return jax.shard_map(
         local,
         mesh=mesh,

time: 273 us -> 63.5 us (0.23); the launches traced: 270 us -> 63 us
  waiting for transfers between devices: 143 us -> 0 us
  Pallas kernels: 0 us -> 52.8 us
  matrix products: 35.8 us -> 0 us
  local copies, waits for them, and re-layouts: 36.1 us -> 7.86 us
  blocking collectives: 18.6 us -> 0 us
  between operations: 14.6 us -> 0.71 us
  other arithmetic: 15.1 us -> 1.65 us
  loops' own time: 5.91 us -> 0 us
    reduce_scatter x1 -> x0, waiting for transfers between devices: 64.7 us -> none  [local(): lax.psum_scatter(local_term, 'shard', scatter_dimension=0, tiled=True)]
    pallas_call x0 -> x3, Pallas kernels: none -> 52.8 us  [the longest x1 43.8 us: kernel_local(): pl.pallas_call(functools.partial(exchange_kernel, shards, reps, norm_limi...]
    all_gather x1 -> x0, waiting for transfers between devices: 45.8 us -> none  [local(): lax.all_gather(new_params.astype(jnp.bfloat16), 'shard', axis=1, tiled=True)]
    dot_general x18 -> x0, matrix products: 35.8 us -> none  [the longest x8 17.5 us: select_rows(): return jnp.dot(selector, node_rows, preferred_element_type=jnp.float32)]
    psum x1 -> x0, waiting for transfers between devices: 32.8 us -> none  [local(): summed = lax.psum(summed, 'rep')]
    dynamic_slice x24 -> x0, local copies, waits for them, and re-layouts: 26.8 us -> none  [local(): lax.map(system_product, (node_feat, node_cot, edge_length, atom_count, ed...]
    psum x1 -> x0, blocking collectives: 18.6 us -> none  [local(): square_sum = lax.psum(jnp.sum(gradients * gradients), 'shard')]
    div x8 -> x1, other arithmetic: 6.63 us -> 0.07 us  [mixing_table(): return product_table / jnp.sum(product_table, axis=1, keepdims=True)]
  transfers between devices with their start and end apart: 3 -> 0, of which waited for: 3 -> 0; matrix products, arithmetic and copies ran while one was open for 1% -> 0% of each run, Pallas kernels for 0% -> 0%
where the time goes in v1:
time: 63.5 us; the launch traced here: 63 us
  Pallas kernels  52.8 us (83%)
  local copies, waits for them, and re-layouts  7.86 us (12%)
  other arithmetic  1.65 us (3%)
  between operations  0.71 us (1%)
    pallas_call x1, Pallas kernels, kernel_local(): pl.pallas_call(functools.partial(exchange_kernel, shards, reps, norm_limi...  43.8 us
    unnamed x26, local copies, waits for them, and re-layouts  7.77 us
    pallas_call x1, Pallas kernels, kernel_local(): pl.pallas_call(functools.partial(partial_kernel, charge_gain.shape[0], sp...  5.53 us
    pallas_call x1, Pallas kernels, kernel_local(): pl.pallas_call(finish_kernel, grid=(steps,), out_shape=(state, state, sta...  3.45 us

profile of v1, /device:TPU:1, one launch (start us, length us, event | category | flops | bytes accessed | tf_op | source)
XLA Modules:
  0.0 63.0 jit_solution(4687662007902416978)
XLA Ops:
  0.6 0.0 copy-start.2
  0.6 0.0 copy-start.1
  0.7 0.0 copy-start
  0.7 0.8 %broadcast_multiply_fusion.1 = f32[2,2,32]{2,1,0:T(2,128)S(1)} fusion(f32[2,32]{1,0:T(2,128)} %param.27, f32[2,32]{1,0:T(2,128)} %param.26), kind=kLoop, calls=%fused_computation.2 | loop fusion | flops 128 | bytes 1024 | tf_op jit(solution)/shard_map/mul | solution.py:29
  1.5 0.8 %fusion = (f32[2,2,2]{2,1,0:T(2,128)S(1)}, f32[2,2,2,32]{3,2,1,0:T(2,128)S(1)}) fusion(f32[2,32]{1,0:T(2,128)} %param.28, f32[2,2,32]{2,1,0:T(2,128)S(1)} %broadcast_multiply_fusion.1), kind=kLoop, calls=%fused_computation.3 | loop fusion | flops 504 | bytes 1824 | tf_op jit(solution)/shard_map/reduce_sum | solution.py:32
  2.2 0.1 div.10
  2.3 0.1 broadcast_divide_fusion.mixing
  2.4 0.0 copy-start.3
  2.4 1.0 %copy-done.3 = bf16[8,128,256]{2,1,0:T(8,128)(2,1)S(1)} copy-done((bf16[8,128,256]{2,1,0:T(8,128)(2,1)S(1)}, bf16[8,128,256]{2,1,0:T(8,128)(2,1)}, u32[]{:S(2)}) %copy-start.3) | copy-done | bytes 524312
  3.5 0.0 copy-start.4
  3.5 1.0 %copy-done.4 = bf16[8,128,256]{2,1,0:T(8,128)(2,1)S(1)} copy-done((bf16[8,128,256]{2,1,0:T(8,128)(2,1)S(1)}, bf16[8,128,256]{2,1,0:T(8,128)(2,1)}, u32[]{:S(2)}) %copy-start.4) | copy-done | bytes 524312
  4.5 0.0 copy-start.5
  4.5 0.8 %copy-done.5 = f32[8,1536]{1,0:T(8,128)S(1)} copy-done((f32[8,1536]{1,0:T(8,128)S(1)}, f32[8,1536]{1,0:T(8,128)}, u32[]{:S(2)}) %copy-start.5) | copy-done | bytes 49176
  5.3 0.0 copy-start.6
  5.3 0.8 %copy-done.6 = s32[8,1536]{1,0:T(8,128)S(1)} copy-done((s32[8,1536]{1,0:T(8,128)S(1)}, s32[8,1536]{1,0:T(8,128)}, u32[]{:S(2)}) %copy-start.6) | copy-done | bytes 49176
  6.1 0.0 copy-start.7
  6.1 0.8 %copy-done.7 = s32[8,1536]{1,0:T(8,128)S(1)} copy-done((s32[8,1536]{1,0:T(8,128)S(1)}, s32[8,1536]{1,0:T(8,128)}, u32[]{:S(2)}) %copy-start.7) | copy-done | bytes 49176
  6.9 0.0 copy-start.8
  6.9 0.7 %copy-done.8 = s32[8]{0:T(128)S(1)} copy-done((s32[8]{0:T(128)S(1)}, s32[8]{0:T(128)}, u32[]{:S(2)}) %copy-start.8) | copy-done | bytes 56
  7.5 0.0 copy-start.9
  7.5 0.7 %copy-done.9 = s32[8]{0:T(128)S(1)} copy-done((s32[8]{0:T(128)S(1)}, s32[8]{0:T(128)}, u32[]{:S(2)}) %copy-start.9) | copy-done | bytes 56
  8.2 0.0 copy-start.10
  8.2 0.7 %copy-done.10 = s32[8]{0:T(128)S(1)} copy-done((s32[8]{0:T(128)S(1)}, s32[8]{0:T(128)}, u32[]{:S(2)}) %copy-start.10) | copy-done | bytes 56
  8.9 0.0 copy-start.11
  8.9 0.7 %copy-done.11 = s32[8]{0:T(128)S(1)} copy-done((s32[8]{0:T(128)S(1)}, s32[8]{0:T(128)}, u32[]{:S(2)}) %copy-start.11) | copy-done | bytes 56
  9.5 0.0 copy-start.12
  9.5 0.7 %copy-done.12 = s32[8]{0:T(128)S(1)} copy-done((s32[8]{0:T(128)S(1)}, s32[8]{0:T(128)}, u32[]{:S(2)}) %copy-start.12) | copy-done | bytes 56
  10.2 5.5 %partial_sums.1.pieces = bf16[2,2,8,64,128]{4,3,2,1,0:T(8,128)(2,1)S(1)} custom-call(bf16[8,128,256]{2,1,0:T(8,128)(2,1)S(1)} %copy-done.3, bf16[8,128,256]{2,1,0:T(8,128)(2,1)S(1)} %copy-done.4, f32[8,1536]{1,0:T(8,128)S(1)} %copy-done.5, s32[8]{0:T(128)S(1)} %copy-done.8, s32[8]{0:T(128)S(1)} %copy-done.9, s32[8,1536]{1,0:T(8,128)S(1)} %copy-done.6, ...), custom_call_target="tpu_custom_call" | custom-call | tf_op jit(solution)/shard_map/partial_sums/pallas_call | solution.py:413
  15.7 0.0 copy-done.2
  15.7 0.0 copy-done.1
  15.7 0.0 copy-done
  15.7 43.8 %exchange.1 = (f32[4,8,8,128]{3,2,1,0:T(8,128)S(1)}, f32[8,128]{1,0:T(8,128)S(1)}, bf16[32,256,128]{2,1,0:T(8,128)(2,1)S(1)}) custom-call(f32[8,32]{1,0:T(8,128)S(1)} %broadcast_divide_fusion.mixing, bf16[2,2,8,64,128]{4,3,2,1,0:T(8,128)(2,1)S(1)} %partial_sums.1.pieces, f32[32,4,8,128]{3,2,1,0:T(8,128)S(1)} %bitcast.8, f32[32,4,8,128]{3,2,1,0:T(8,128)S(1)} %bitcast.10, ...), custom_call_target="tpu_custom_call" | custom-call | tf_op jit(solution)/shard_map/exchange/pallas_call | solution.py:429
  59.6 3.4 %finish.1 = (f32[32,4,8,128]{3,2,1,0:T(8,128)}, f32[32,4,8,128]{3,2,1,0:T(8,128)}, f32[32,4,8,128]{3,2,1,0:T(8,128)}, bf16[32,256,128]{2,1,0:T(8,128)(2,1)}) custom-call(f32[8,32]{1,0:T(8,128)S(1)} %broadcast_divide_fusion.mixing, f32[4,8,8,128]{3,2,1,0:T(8,128)S(1)} %get-tuple-element.11.summed, f32[8,128]{1,0:T(8,128)S(1)} %get-tuple-element.12.clip, ...), custom_call_target="tpu_custom_call" | custom-call | tf_op jit(solution)/shard_map/finish/pallas_call | solution.py:469
Async XLA Ops:
  0.6 15.1 %copy-start.2 = (f32[32,16,2,128]{3,2,1,0:T(2,128)S(1)}, f32[32,16,2,128]{3,2,1,0:T(2,128)}, u32[]{:S(2)}) copy-start(f32[32,16,2,128]{3,2,1,0:T(2,128)} %param.31) | copy-start | bytes 1572868
  0.6 15.1 %copy-start.1 = (f32[32,16,2,128]{3,2,1,0:T(2,128)S(1)}, f32[32,16,2,128]{3,2,1,0:T(2,128)}, u32[]{:S(2)}) copy-start(f32[32,16,2,128]{3,2,1,0:T(2,128)} %param.30) | copy-start | bytes 1572868
  0.7 15.1 %copy-start = (f32[32,16,2,128]{3,2,1,0:T(2,128)S(1)}, f32[32,16,2,128]{3,2,1,0:T(2,128)}, u32[]{:S(2)}) copy-start(f32[32,16,2,128]{3,2,1,0:T(2,128)} %param.29) | copy-start | bytes 1572868
  2.4 1.0 %copy-start.3 = (bf16[8,128,256]{2,1,0:T(8,128)(2,1)S(1)}, bf16[8,128,256]{2,1,0:T(8,128)(2,1)}, u32[]{:S(2)}) copy-start(bf16[8,128,256]{2,1,0:T(8,128)(2,1)} %feat.1) | copy-start | bytes 1572868
  3.5 1.0 %copy-start.4 = (bf16[8,128,256]{2,1,0:T(8,128)(2,1)S(1)}, bf16[8,128,256]{2,1,0:T(8,128)(2,1)}, u32[]{:S(2)}) copy-start(bf16[8,128,256]{2,1,0:T(8,128)(2,1)} %cot.1) | copy-start | bytes 1572868
  4.5 0.8 %copy-start.5 = (f32[8,1536]{1,0:T(8,128)S(1)}, f32[8,1536]{1,0:T(8,128)}, u32[]{:S(2)}) copy-start(f32[8,1536]{1,0:T(8,128)} %length.1) | copy-start | bytes 147460
  5.3 0.8 %copy-start.6 = (s32[8,1536]{1,0:T(8,128)S(1)}, s32[8,1536]{1,0:T(8,128)}, u32[]{:S(2)}) copy-start(s32[8,1536]{1,0:T(8,128)} %source.1) | copy-start | bytes 147460
  6.1 0.8 %copy-start.7 = (s32[8,1536]{1,0:T(8,128)S(1)}, s32[8,1536]{1,0:T(8,128)}, u32[]{:S(2)}) copy-start(s32[8,1536]{1,0:T(8,128)} %target.1) | copy-start | bytes 147460
  6.9 0.7 %copy-start.8 = (s32[8]{0:T(128)S(1)}, s32[8]{0:T(128)}, u32[]{:S(2)}) copy-start(s32[8]{0:T(128)} %atoms.1) | copy-start | bytes 100
  7.5 0.7 %copy-start.9 = (s32[8]{0:T(128)S(1)}, s32[8]{0:T(128)}, u32[]{:S(2)}) copy-start(s32[8]{0:T(128)} %edges.1) | copy-start | bytes 100
  8.2 0.7 %copy-start.10 = (s32[8]{0:T(128)S(1)}, s32[8]{0:T(128)}, u32[]{:S(2)}) copy-start(s32[8]{0:T(128)} %dataset.1) | copy-start | bytes 100
  8.9 0.7 %copy-start.11 = (s32[8]{0:T(128)S(1)}, s32[8]{0:T(128)}, u32[]{:S(2)}) copy-start(s32[8]{0:T(128)} %charge.1) | copy-start | bytes 100
  9.5 0.7 %copy-start.12 = (s32[8]{0:T(128)S(1)}, s32[8]{0:T(128)}, u32[]{:S(2)}) copy-start(s32[8]{0:T(128)} %spin.1) | copy-start | bytes 100

commit v2 on v0

--- a/solution.py
+++ b/solution.py
@@ -1,8 +1,11 @@
+import functools
 import math
 
 import jax
 import jax.numpy as jnp
 from jax import lax
+from jax.experimental import pallas as pl
+from jax.experimental.pallas import tpu as pltpu
 from jax.sharding import PartitionSpec as P
 
 STEP = 10
@@ -69,7 +72,7 @@
     return (new_params, new_one, new_two)
 
 
-def local(
+def plain_local(
     node_feat,
     node_cot,
     edge_length,
@@ -114,6 +117,435 @@
     return (new_params, new_one, new_two, full_weights)
 
 
+MIB = 1024 * 1024
+MESH = pl.DeviceIdType.MESH
+
+
+def split_dot(left, right, contract):
+    high = right.astype(jnp.bfloat16)
+    low = (right - high.astype(jnp.float32)).astype(jnp.bfloat16)
+    dims = (contract, ((), ()))
+    return lax.dot_general(
+        left, high, dims, preferred_element_type=jnp.float32
+    ) + lax.dot_general(left, low, dims, preferred_element_type=jnp.float32)
+
+
+def split_dot_left(left, right):
+    high = left.astype(jnp.bfloat16)
+    low = (left - high.astype(jnp.float32)).astype(jnp.bfloat16)
+    dims = (((0,), (0,)), ((), ()))
+    return lax.dot_general(
+        high, right, dims, preferred_element_type=jnp.float32
+    ) + lax.dot_general(low, right, dims, preferred_element_type=jnp.float32)
+
+
+def expert_rows(mixing, summed, expert):
+    total = mixing[0, expert] * summed[:, 0]
+    for k in range(1, summed.shape[1]):
+        total = total + mixing[k, expert] * summed[:, k]
+    return total
+
+
+def adam_rows(gradient, clip, params, moment_one, moment_two):
+    clipped = clip * gradient
+    new_one = beta_one * moment_one + (1.0 - beta_one) * clipped
+    new_two = beta_two * moment_two + (1.0 - beta_two) * clipped * clipped
+    first_fix = 1.0 - beta_one**STEP
+    second_fix = 1.0 - beta_two**STEP
+    direction = new_one / first_fix / (jnp.sqrt(new_two / second_fix) + adam_eps)
+    return params - learn_rate * (direction + decay_rate * params), new_one, new_two
+
+
+def system_sums(feat, cot, weight, source, target, atoms, edges, products):
+    systems, slots, width = feat.shape
+    channels = width // 2
+    lanes = source.shape[1]
+
+    def one_system(s, carry):
+        slot_index = lax.broadcasted_iota(jnp.int32, (1, lanes), 1)
+        atom_index = lax.broadcasted_iota(jnp.int32, (slots, lanes), 0)
+        count = jnp.full((1, lanes), atoms[s], jnp.int32).astype(jnp.float32)
+        factor = jnp.where(slot_index < edges[s], float(slots) / count, 0.0)
+        row = weight[pl.ds(s, 1), :] * factor
+        left = jnp.where(atom_index == source[pl.ds(s, 1), :], row, 0.0).astype(jnp.bfloat16)
+        right = jnp.where(atom_index == target[pl.ds(s, 1), :], 1.0, 0.0).astype(jnp.bfloat16)
+        pairs = lax.dot_general(
+            right, left, (((1,), (1,)), ((), ())), preferred_element_type=jnp.float32
+        )
+        mixed = split_dot_left(pairs, cot[s])
+        real, imag = mixed[:, :channels], mixed[:, channels:]
+        block = jnp.concatenate(
+            [
+                jnp.concatenate([real, imag], axis=1),
+                jnp.concatenate([imag, -real], axis=1),
+            ],
+            axis=0,
+        )
+        rows = feat[s]
+        stacked = jnp.concatenate([rows[:, :channels], rows[:, channels:]], axis=0)
+        product = split_dot(stacked, block, ((0,), (0,)))
+        products[s, pl.ds(0, channels, stride=2), :] = product[:, :channels]
+        products[s, pl.ds(1, channels, stride=2), :] = product[:, channels:]
+        return carry
+
+    lax.fori_loop(0, systems, one_system, 0, unroll=UNROLL_SYSTEMS)
+
+
+UNROLL_SYSTEMS = 4
+
+
+def whole_kernel(
+    shards, reps, norm_limit,
+    feat_in, cot_in, length_in, atoms_in, edges_in, source_in, target_in,
+    dataset_in, charge_in, spin_in, dataset_gain_in, charge_gain_in, spin_gain_in,
+    params_in, one_in, two_in,
+    new_params_out, new_one_out, new_two_out, weights,
+    feat, cot, length, source, target, dataset_gain, charge_gain, spin_gain,
+    params, moment_one, moment_two, new_params, new_one, new_two, table, atoms, edges, dataset, charge, spin, mixing,
+    products, pieces, pair_in, pair_sum, slices, summed, norms,
+    fetch_sem, store_sem, table_sem, pair_sem, slice_send, slice_recv, rep_send, rep_recv,
+    norm_send, norm_recv, z_send, z_recv, y_send, y_recv, x_send, x_recv, core_send, core_recv,
+):
+    shard, rep = lax.axis_index("shard"), lax.axis_index("rep")
+    planes, depth = reps // 2, shards // 2
+    x, core = rep // 2, rep % 2
+    z, y = shard // 2, shard % 2
+    devices = shards * reps
+    me = shard * reps + rep
+    experts = params.shape[0]
+    tags = summed.shape[1]
+
+    fetches = [
+        pltpu.make_async_copy(src, dst, fetch_sem.at[i])
+        for i, (src, dst) in enumerate(
+            (
+                (source_in, source), (target_in, target), (length_in, length),
+                (atoms_in, atoms), (edges_in, edges), (cot_in, cot), (feat_in, feat),
+                (dataset_in, dataset), (charge_in, charge), (spin_in, spin),
+                (dataset_gain_in, dataset_gain), (charge_gain_in, charge_gain),
+                (spin_gain_in, spin_gain),
+                (params_in, params), (one_in, moment_one), (two_in, moment_two),
+            )
+        )
+    ]
+    for fetch in fetches:
+        fetch.start()
+
+    barrier = pltpu.get_barrier_semaphore()
+    for j in range(1, devices):
+        other = lax.rem(me + j, devices)
+        pl.semaphore_signal(
+            barrier, inc=1, device_id=(other // reps, lax.rem(other, reps)), device_id_type=MESH
+        )
+
+    for fetch in fetches[:13]:
+        fetch.wait()
+    charges, spins = charge_gain.shape[0], spin_gain.shape[0]
+    table[...] = jnp.zeros_like(table)
+    for k in range(tags):
+        d, c, s = k // (charges * spins), (k // spins) % charges, k % spins
+        line = dataset_gain[d : d + 1, :] * charge_gain[c : c + 1, :] * spin_gain[s : s + 1, :]
+        table[k : k + 1, 0:experts] = line / jnp.sum(line, axis=1, keepdims=True)
+    to_scalars = pltpu.make_async_copy(table, mixing, table_sem)
+    to_scalars.start()
+
+    length[...] = envelope(length[...])
+    system_sums(feat, cot, length, source, target, atoms, edges, products)
+
+    systems, _, channels = products.shape
+    rows_of = [
+        (dataset[s] * charges + charge[s]) * spins + spin[s] for s in range(systems)
+    ]
+    takes = [
+        [jnp.where(rows_of[s] == k, 1.0, 0.0) for s in range(systems)] for k in range(tags)
+    ]
+
+    def group(i, carry):
+        at = pl.multiple_of(i * 8, 8)
+        terms = [products[s, pl.ds(at, 8), :] for s in range(systems)]
+        sums = []
+        for k in range(tags):
+            total = takes[k][0] * terms[0]
+            for s in range(1, systems):
+                total = total + takes[k][s] * terms[s]
+            sums.append(total)
+        owner, r = i // reps, lax.rem(i, reps)
+        pieces[lax.rem(r, 2), r // 2, owner] = jnp.concatenate(sums, axis=0)
+        return carry
+
+    lax.fori_loop(0, devices, group, 0, unroll=2)
+    pl.semaphore_wait(barrier, devices - 1)
+
+    def send(src, dst, send_sem, recv_sem, to):
+        copy = pltpu.make_async_remote_copy(
+            src_ref=src, dst_ref=dst, send_sem=send_sem, recv_sem=recv_sem,
+            device_id=to, device_id_type=MESH,
+        )
+        copy.start()
+        return copy
+
+    sibling = (shard, x * 2 + 1 - core)
+    started = []
+
+    order = [(dx, lax.rem(x + dx, planes)) for dx in range(planes - 1, -1, -1)]
+    pair = [
+        send(
+            pieces.at[1 - core, i], pair_in.at[i],
+            pair_sem.at[0, dx], pair_sem.at[1, dx], sibling,
+        )
+        for dx, i in order
+    ]
+    started += pair
+    arriving = []
+    for at, (dx, i) in enumerate(order):
+        pair[at].wait_recv()
+        pair_sum[i] = pieces[core, i] + pair_in[i]
+        for ds in range(shards):
+            if ds == 0 and dx == 0:
+                continue
+            to_s = lax.rem(shard + ds, shards)
+            j = dx * shards + ds
+            arriving.append(
+                send(
+                    pair_sum.at[i, to_s], slices.at[j], slice_send.at[j], slice_recv.at[j],
+                    (to_s, i * 2 + core),
+                )
+            )
+    to_scalars.wait()
+    total = pair_sum[x, shard]
+    for copy in arriving:
+        copy.wait_recv()
+    for j in range(1, planes * shards):
+        total = total + slices[j]
+    started += arriving
+    own = total.reshape(tags, 8, total.shape[-1])
+    summed[rep] = own
+
+    shared = []
+    for j in range(1, reps):
+        shared.append(
+            send(
+                summed.at[rep], summed.at[rep], rep_send.at[j], rep_recv.at[j],
+                (shard, lax.rem(rep + j, reps)),
+            )
+        )
+    squares = jnp.zeros(own.shape[1:], jnp.float32)
+    for e in range(experts):
+        gradient = expert_rows(mixing, own[None], e)[0]
+        squares = squares + gradient * gradient
+    norms[me] = squares
+    normed = []
+    for j in range(1, devices):
+        other = lax.rem(me + j, devices)
+        normed.append(
+            send(
+                norms.at[me], norms.at[me], norm_send.at[j], norm_recv.at[j],
+                (other // reps, lax.rem(other, reps)),
+            )
+        )
+    for fetch in fetches[13:]:
+        fetch.wait()
+    for copy in shared:
+        copy.wait_recv()
+    for copy in normed:
+        copy.wait_recv()
+    started += shared + normed
+    square_sum = jnp.sum(jnp.sum(norms[...], axis=0), axis=(0, 1), keepdims=True)
+    clip = jnp.minimum(1.0, norm_limit / (jnp.sqrt(square_sum) + 1e-06))
+
+    half = experts // 2
+    span = (half * 5) // 8
+    cross = half - span
+    first = core * half + x * cross
+    chunks = (
+        (core * half + x * span, cross, True),
+        (core * half + cross, span - cross, False),
+    )
+    cross_other = core * half + (1 - x) * span
+    rows = weights.shape[1] // shards
+
+    def update(begin):
+        def one(i, carry):
+            e = lax.rem(begin + i, experts)
+            new_params[e], new_one[e], new_two[e] = adam_rows(
+                expert_rows(mixing, summed, e), clip, params[e], moment_one[e], moment_two[e]
+            )
+            weights[e, pl.ds(pl.multiple_of(shard * rows, rows), rows), :] = (
+                new_params[e].reshape(rows, weights.shape[-1]).astype(jnp.bfloat16)
+            )
+            return carry
+
+        return one
+
+    def pass_on(begin, count, owner, send_sem, recv_sem, to):
+        block = weights.at[
+            pl.ds(begin, count), pl.ds(pl.multiple_of(owner * rows, rows), rows), :
+        ]
+        copy = send(block, block, send_sem, recv_sem, to)
+        started.append(copy)
+        return copy
+
+    beside = (z * 2 + 1 - y, rep)
+    across = (shard, (1 - x) * 2 + core)
+    along = [[None] * depth for _ in chunks]
+    turned = [[None] * depth for _ in chunks]
+    for n, (begin, count, _) in enumerate(chunks):
+        lax.fori_loop(0, count, update(begin), 0, unroll=count)
+        for d in range(1, depth):
+            to = lax.rem(z + d, depth) * 2 + y
+            along[n][d] = pass_on(
+                begin, count, shard, z_send.at[n, d], z_recv.at[n, d], (to, rep)
+            )
+        turned[n][0] = pass_on(begin, count, shard, y_send.at[n, 0], y_recv.at[n, 0], beside)
+    lax.fori_loop(0, experts - span, update(first + span), 0, unroll=2)
+    stores = [
+        pltpu.make_async_copy(src, dst, store_sem.at[i])
+        for i, (src, dst) in enumerate(
+            ((new_params, new_params_out), (new_one, new_one_out), (new_two, new_two_out))
+        )
+    ]
+    for store in stores:
+        store.start()
+
+    crossed, paired = [], []
+
+    def arrived(n, slot, owner):
+        begin, count, crosses = chunks[n]
+        if crosses:
+            copy = pass_on(begin, count, owner, x_send.at[slot], x_recv.at[slot], across)
+            crossed.append((slot, owner, copy))
+        paired.append(
+            pass_on(begin, count, owner, core_send.at[n, slot], core_recv.at[n, slot], sibling)
+        )
+
+    def from_across():
+        slot, owner, copy = crossed.pop(0)
+        copy.wait_recv()
+        paired.append(
+            pass_on(
+                cross_other, cross, owner,
+                core_send.at[len(chunks), slot], core_recv.at[len(chunks), slot], sibling,
+            )
+        )
+
+    for n, (begin, count, _) in enumerate(chunks):
+        turned[n][0].wait_recv()
+        arrived(n, depth, z * 2 + 1 - y)
+        for d in range(1, depth):
+            along[n][d].wait_recv()
+            owner = lax.rem(z + depth - d, depth) * 2 + y
+            turned[n][d] = pass_on(
+                begin, count, owner, y_send.at[n, d], y_recv.at[n, d], beside
+            )
+            arrived(n, d, owner)
+        if n == 0:
+            continue
+        for d in range(1, depth):
+            turned[n - 1][d].wait_recv()
+            arrived(n - 1, depth + d, lax.rem(z + depth - d, depth) * 2 + 1 - y)
+    for _ in range(depth):
+        from_across()
+    for d in range(1, depth):
+        turned[-1][d].wait_recv()
+        arrived(len(chunks) - 1, depth + d, lax.rem(z + depth - d, depth) * 2 + 1 - y)
+    while crossed:
+        from_across()
+    for copy in paired:
+        copy.wait_recv()
+    for copy in started:
+        copy.wait_send()
+    for store in stores:
+        store.wait()
+
+
+def finish_kernel(*refs):
+    count = (len(refs) - 1) // 2
+    sem = refs[-1]
+    copies = [
+        pltpu.make_async_copy(refs[i], refs[count + i], sem.at[i]) for i in range(count)
+    ]
+    for copy in copies:
+        copy.start()
+    for copy in copies:
+        copy.wait()
+
+
+def kernel_local(shards, reps, *args):
+    params = args[13]
+    experts, own_channels, parts, channels = params.shape
+    planes, depth, devices = reps // 2, shards // 2, shards * reps
+    f32, bf16, i32 = jnp.float32, jnp.bfloat16, jnp.int32
+    dma = pltpu.SemaphoreType.DMA
+    anywhere = pl.BlockSpec(memory_space=pl.ANY)
+    vmem = pl.BlockSpec(memory_space=pltpu.VMEM)
+    systems, lanes = args[2].shape
+    gains = args[10:13]
+    tags = gains[0].shape[0] * gains[1].shape[0] * gains[2].shape[0]
+    slice_rows = tags * 8
+    rows = own_channels * parts
+    states = [a.reshape(experts, reps, 8, channels) for a in args[13:16]]
+    state = (experts, reps, 8, channels)
+    norm_limit = math.sqrt(experts * parts * channels * channels)
+    chunk_total = 2
+
+    def held(array):
+        return pltpu.VMEM(array.shape, array.dtype)
+
+    def pairs(*shape):
+        return [dma(shape), dma(shape)]
+
+    outs = [jax.ShapeDtypeStruct(state, f32)] * 3
+    outs.append(jax.ShapeDtypeStruct((experts, shards * rows, channels), bf16))
+    results = pl.pallas_call(
+        functools.partial(whole_kernel, shards, reps, norm_limit),
+        out_shape=outs,
+        in_specs=[anywhere] * 16,
+        out_specs=[anywhere] * 3 + [vmem],
+        scratch_shapes=[
+            held(args[0]), held(args[1]), held(args[2]), held(args[5]), held(args[6]),
+            *[held(a) for a in gains],
+            *[pltpu.VMEM(state, f32)] * 6,
+            pltpu.VMEM((tags, 128), f32),
+            *[pltpu.SMEM((systems,), i32)] * 5,
+            pltpu.SMEM((tags, 128), f32),
+            pltpu.VMEM((systems, channels * parts, channels), f32),
+            pltpu.VMEM((2, planes, shards, slice_rows, channels), f32),
+            pltpu.VMEM((planes, shards, slice_rows, channels), f32),
+            pltpu.VMEM((planes, shards, slice_rows, channels), f32),
+            pltpu.VMEM((planes * shards, slice_rows, channels), f32),
+            pltpu.VMEM((reps, tags, 8, channels), f32),
+            pltpu.VMEM((devices, 8, channels), f32),
+            dma((16,)),
+            dma((3,)),
+            dma,
+            dma((2, planes)),
+            *pairs(planes * shards),
+            *pairs(reps),
+            *pairs(devices),
+            *pairs(chunk_total, depth),
+            *pairs(chunk_total, depth),
+            *pairs(shards),
+            *pairs(chunk_total + 1, shards),
+        ],
+        compiler_params=pltpu.CompilerParams(
+            collective_id=0, has_side_effects=True, vmem_limit_bytes=60 * MIB
+        ),
+        name="whole",
+    )(*args[:13], *states)
+
+    outs = pl.pallas_call(
+        finish_kernel,
+        out_shape=outs,
+        in_specs=[anywhere] * 4,
+        out_specs=[anywhere] * 4,
+        scratch_shapes=[dma((4,))],
+        compiler_params=pltpu.CompilerParams(vmem_limit_bytes=60 * MIB),
+        name="finish",
+    )(*results)
+    local_states = [a.reshape(params.shape) for a in outs[:3]]
+    return (*local_states, outs[3].reshape(experts, shards * own_channels, parts, channels))
+
+
 def solution(mesh):
     placed = (
         P(("shard", "rep"), None, None),
@@ -133,6 +565,14 @@
         P(None, "shard", None, None),
         P(None, "shard", None, None),
     )
+    shards, reps = mesh.shape["shard"], mesh.shape["rep"]
+
+    def local(*args):
+        params = args[13]
+        if reps == 4 and shards % 2 == 0 and params.shape[1] * params.shape[2] == 8 * reps:
+            return kernel_local(shards, reps, *args)
+        return plain_local(*args)
+
     return jax.shard_map(
         local,
         mesh=mesh,

time: 273 us -> 161 us (0.59); the launches traced: 270 us -> 161 us
  Pallas kernels: 0 us -> 160 us
  waiting for transfers between devices: 143 us -> 0 us
  local copies, waits for them, and re-layouts: 36.1 us -> 0 us
  matrix products: 35.8 us -> 0 us
  blocking collectives: 18.6 us -> 0 us
  other arithmetic: 15.1 us -> 0 us
  between operations: 14.6 us -> 0.65 us
  loops' own time: 5.91 us -> 0 us
    pallas_call x0 -> x2, Pallas kernels: none -> 160 us  [the longest x1 112 us: kernel_local(): pl.pallas_call(finish_kernel, out_shape=outs, in_specs=[anywhere] * 4, ou...]
    reduce_scatter x1 -> x0, waiting for transfers between devices: 64.7 us -> none  [local(): lax.psum_scatter(local_term, 'shard', scatter_dimension=0, tiled=True)]
    all_gather x1 -> x0, waiting for transfers between devices: 45.8 us -> none  [local(): lax.all_gather(new_params.astype(jnp.bfloat16), 'shard', axis=1, tiled=True)]
    dot_general x18 -> x0, matrix products: 35.8 us -> none  [the longest x8 17.5 us: select_rows(): return jnp.dot(selector, node_rows, preferred_element_type=jnp.float32)]
    psum x1 -> x0, waiting for transfers between devices: 32.8 us -> none  [local(): summed = lax.psum(summed, 'rep')]
    dynamic_slice x24 -> x0, local copies, waits for them, and re-layouts: 26.8 us -> none  [local(): lax.map(system_product, (node_feat, node_cot, edge_length, atom_count, ed...]
    psum x1 -> x0, blocking collectives: 18.6 us -> none  [local(): square_sum = lax.psum(jnp.sum(gradients * gradients), 'shard')]
    unnamed x20 -> x0, local copies, waits for them, and re-layouts: 9.22 us -> none
  transfers between devices with their start and end apart: 3 -> 0, of which waited for: 3 -> 0; matrix products, arithmetic and copies ran while one was open for 1% -> 0% of each run, Pallas kernels for 0% -> 0%
where the time goes in v2:
time: 161 us
  Pallas kernels  160 us (99%)
    pallas_call x1, Pallas kernels, kernel_local(): pl.pallas_call(finish_kernel, out_shape=outs, in_specs=[anywhere] * 4, ou...  112 us
    pallas_call x1, Pallas kernels, kernel_local(): pl.pallas_call(functools.partial(whole_kernel, shards, reps, norm_limit),...  47.8 us

profile of v2, /device:TPU:1, one launch (start us, length us, event | category | flops | bytes accessed | tf_op | source)
XLA Modules:
  0.0 160.8 jit_solution(3925999912500987291)
XLA Ops:
  0.6 47.8 %whole.1 = (f32[32,4,8,128]{3,2,1,0:T(8,128)}, f32[32,4,8,128]{3,2,1,0:T(8,128)}, f32[32,4,8,128]{3,2,1,0:T(8,128)}, bf16[32,256,128]{2,1,0:T(8,128)(2,1)}) custom-call(bf16[8,128,256]{2,1,0:T(8,128)(2,1)} %feat_in.1, bf16[8,128,256]{2,1,0:T(8,128)(2,1)} %cot_in.1, f32[8,1536]{1,0:T(8,128)} %length_in.1, s32[8]{0:T(128)} %atoms_in.1, s32[8]{0:T(128)} %edges_in.1, ...), custom_call_target="tpu_custom_call" | custom-call | tf_op jit(solution)/shard_map/whole/pallas_call | solution.py:499
  48.4 112.3 %finish.1 = (f32[32,4,8,128]{3,2,1,0:T(8,128)}, f32[32,4,8,128]{3,2,1,0:T(8,128)}, f32[32,4,8,128]{3,2,1,0:T(8,128)}, bf16[32,256,128]{2,1,0:T(8,128)(2,1)}) custom-call(f32[32,4,8,128]{3,2,1,0:T(8,128)} %get-tuple-element.12.refs_0_, f32[32,4,8,128]{3,2,1,0:T(8,128)} %get-tuple-element.13.refs_1_, f32[32,4,8,128]{3,2,1,0:T(8,128)} %get-tuple-element.14.refs_2_, ...), custom_call_target="tpu_custom_call" | custom-call | tf_op jit(solution)/shard_map/finish/pallas_call | solution.py:536

commit v3 on v2

--- a/solution.py
+++ b/solution.py
@@ -202,8 +202,8 @@
     new_params_out, new_one_out, new_two_out, weights,
     feat, cot, length, source, target, dataset_gain, charge_gain, spin_gain,
     params, moment_one, moment_two, new_params, new_one, new_two, table, atoms, edges, dataset, charge, spin, mixing,
-    products, pieces, pair_in, pair_sum, slices, summed, norms,
-    fetch_sem, store_sem, table_sem, pair_sem, slice_send, slice_recv, rep_send, rep_recv,
+    products, pieces, pair_in, pair_sum, slices, z_sum, z_in, summed, norms,
+    fetch_sem, store_sem, table_sem, pair_sem, slice_send, slice_recv, ahead_send, ahead_recv, rep_send, rep_recv,
     norm_send, norm_recv, z_send, z_recv, y_send, y_recv, x_send, x_recv, core_send, core_recv,
 ):
     shard, rep = lax.axis_index("shard"), lax.axis_index("rep")
@@ -287,37 +287,44 @@
     sibling = (shard, x * 2 + 1 - core)
     started = []
 
-    order = [(dx, lax.rem(x + dx, planes)) for dx in range(planes - 1, -1, -1)]
-    pair = [
-        send(
-            pieces.at[1 - core, i], pair_in.at[i],
-            pair_sem.at[0, dx], pair_sem.at[1, dx], sibling,
-        )
-        for dx, i in order
-    ]
-    started += pair
-    arriving = []
-    for at, (dx, i) in enumerate(order):
-        pair[at].wait_recv()
-        pair_sum[i] = pieces[core, i] + pair_in[i]
-        for ds in range(shards):
-            if ds == 0 and dx == 0:
-                continue
-            to_s = lax.rem(shard + ds, shards)
-            j = dx * shards + ds
-            arriving.append(
+    parts = [(dz, lax.rem(z + dz, depth)) for dz in [*range(1, depth), 0]]
+    sides = [(dx, dy) for dx in range(planes) for dy in range(2) if (dx, dy) != (0, 0)]
+    pair, sided, ahead = {}, {}, []
+    for dz, to_z in parts:
+        both = pl.ds(pl.multiple_of(to_z * 2, 2), 2)
+        pair[dz] = send(
+            pieces.at[1 - core, :, both], pair_in.at[:, both],
+            pair_sem.at[0, dz], pair_sem.at[1, dz], sibling,
+        )
+    for dz, to_z in parts:
+        both = pl.ds(pl.multiple_of(to_z * 2, 2), 2)
+        pair[dz].wait_recv()
+        pair_sum[:, both] = pieces[core, :, both] + pair_in[:, both]
+        for n, (dx, dy) in enumerate(sides):
+            to_x, to_y = lax.rem(x + dx, planes), lax.rem(y + dy, 2)
+            sided[dz, n] = send(
+                pair_sum.at[to_x, to_z * 2 + to_y], slices.at[dz, n],
+                slice_send.at[dz, n], slice_recv.at[dz, n],
+                (z * 2 + to_y, to_x * 2 + core),
+            )
+    for dz, to_z in parts:
+        total = pair_sum[x, to_z * 2 + y]
+        for n in range(len(sides)):
+            sided[dz, n].wait_recv()
+            total = total + slices[dz, n]
+        if dz > 0:
+            z_sum[dz] = total
+            ahead.append(
                 send(
-                    pair_sum.at[i, to_s], slices.at[j], slice_send.at[j], slice_recv.at[j],
-                    (to_s, i * 2 + core),
+                    z_sum.at[dz], z_in.at[dz], ahead_send.at[dz], ahead_recv.at[dz],
+                    (to_z * 2 + y, rep),
                 )
             )
     to_scalars.wait()
-    total = pair_sum[x, shard]
-    for copy in arriving:
+    for n, copy in enumerate(ahead):
         copy.wait_recv()
-    for j in range(1, planes * shards):
-        total = total + slices[j]
-    started += arriving
+        total = total + z_in[n + 1]
+    started += [*pair.values(), *sided.values(), *ahead]
     own = total.reshape(tags, 8, total.shape[-1])
     summed[rep] = own
 
@@ -459,15 +466,30 @@
 
 
 def finish_kernel(*refs):
-    count = (len(refs) - 1) // 2
-    sem = refs[-1]
-    copies = [
-        pltpu.make_async_copy(refs[i], refs[count + i], sem.at[i]) for i in range(count)
-    ]
-    for copy in copies:
-        copy.start()
-    for copy in copies:
-        copy.wait()
+    count = (len(refs) - 2) // 3
+    load_sem, store_sem = refs[-2:]
+    loads, stores = [], []
+    for i in range(count):
+        source, result, held = refs[i], refs[count + i], refs[2 * count + i]
+        rows = source.shape[0] // FINISH_PARTS
+        for n in range(FINISH_PARTS):
+            block = pl.ds(n * rows, rows)
+            loads.append(
+                pltpu.make_async_copy(source.at[block], held.at[block], load_sem.at[i, n])
+            )
+            stores.append(
+                pltpu.make_async_copy(held.at[block], result.at[block], store_sem.at[i, n])
+            )
+    for load in loads:
+        load.start()
+    for load, store in zip(loads, stores):
+        load.wait()
+        store.start()
+    for store in stores:
+        store.wait()
+
+
+FINISH_PARTS = 4
 
 
 def kernel_local(shards, reps, *args):
@@ -512,14 +534,17 @@
             pltpu.VMEM((2, planes, shards, slice_rows, channels), f32),
             pltpu.VMEM((planes, shards, slice_rows, channels), f32),
             pltpu.VMEM((planes, shards, slice_rows, channels), f32),
-            pltpu.VMEM((planes * shards, slice_rows, channels), f32),
+            pltpu.VMEM((depth, planes * 2 - 1, slice_rows, channels), f32),
+            pltpu.VMEM((depth, slice_rows, channels), f32),
+            pltpu.VMEM((depth, slice_rows, channels), f32),
             pltpu.VMEM((reps, tags, 8, channels), f32),
             pltpu.VMEM((devices, 8, channels), f32),
             dma((16,)),
             dma((3,)),
             dma,
-            dma((2, planes)),
-            *pairs(planes * shards),
+            dma((2, depth)),
+            *pairs(depth, planes * 2 - 1),
+            *pairs(depth),
             *pairs(reps),
             *pairs(devices),
             *pairs(chunk_total, depth),
@@ -538,7 +563,7 @@
         out_shape=outs,
         in_specs=[anywhere] * 4,
         out_specs=[anywhere] * 4,
-        scratch_shapes=[dma((4,))],
+        scratch_shapes=[*[held(a) for a in outs], *pairs(4, FINISH_PARTS)],
         compiler_params=pltpu.CompilerParams(vmem_limit_bytes=60 * MIB),
         name="finish",
     )(*results)

time: 161 us -> 49.2 us (0.31)
  Pallas kernels: 160 us -> 48.4 us
    pallas_call x1, Pallas kernels: 112 us -> 3.86 us  [kernel_local(): pl.pallas_call(finish_kernel, out_shape=outs, in_specs=[anywhere] * 4, ou...]
    pallas_call x1, Pallas kernels: 47.8 us -> 44.6 us  [kernel_local(): pl.pallas_call(functools.partial(whole_kernel, shards, reps, norm_limit),...]
where the time goes in v3:
time: 49.2 us; the launch traced here: 49.1 us
  Pallas kernels  48.4 us (98%)
  between operations  0.65 us (1%)
    pallas_call x1, Pallas kernels, kernel_local(): pl.pallas_call(functools.partial(whole_kernel, shards, reps, norm_limit),...  44.6 us
    pallas_call x1, Pallas kernels, kernel_local(): pl.pallas_call(finish_kernel, out_shape=outs, in_specs=[anywhere] * 4, ou...  3.86 us

profile of v3, /device:TPU:1, one launch (start us, length us, event | category | flops | bytes accessed | tf_op | source)
XLA Modules:
  0.0 49.1 jit_solution(13578082771984597330)
XLA Ops:
  0.6 44.6 %whole.1 = (f32[32,4,8,128]{3,2,1,0:T(8,128)}, f32[32,4,8,128]{3,2,1,0:T(8,128)}, f32[32,4,8,128]{3,2,1,0:T(8,128)}, bf16[32,256,128]{2,1,0:T(8,128)(2,1)}) custom-call(bf16[8,128,256]{2,1,0:T(8,128)(2,1)} %feat_in.1, bf16[8,128,256]{2,1,0:T(8,128)(2,1)} %cot_in.1, f32[8,1536]{1,0:T(8,128)} %length_in.1, s32[8]{0:T(128)} %atoms_in.1, s32[8]{0:T(128)} %edges_in.1, ...), custom_call_target="tpu_custom_call" | custom-call | tf_op jit(solution)/shard_map/whole/pallas_call | solution.py:521
  45.2 3.9 %finish.1 = (f32[32,4,8,128]{3,2,1,0:T(8,128)}, f32[32,4,8,128]{3,2,1,0:T(8,128)}, f32[32,4,8,128]{3,2,1,0:T(8,128)}, bf16[32,256,128]{2,1,0:T(8,128)(2,1)}) custom-call(f32[32,4,8,128]{3,2,1,0:T(8,128)} %get-tuple-element.12.refs_0_, f32[32,4,8,128]{3,2,1,0:T(8,128)} %get-tuple-element.13.refs_1_, f32[32,4,8,128]{3,2,1,0:T(8,128)} %get-tuple-element.14.refs_2_, ...), custom_call_target="tpu_custom_call" | custom-call | tf_op jit(solution)/shard_map/finish/pallas_call | solution.py:561

commit v4 on v3

--- a/solution.py
+++ b/solution.py
@@ -192,6 +192,7 @@
 
 
 UNROLL_SYSTEMS = 4
+CROSS_PARTS = 2
 
 
 def whole_kernel(
@@ -364,10 +365,10 @@
     span = (half * 5) // 8
     cross = half - span
     first = core * half + x * cross
-    chunks = (
-        (core * half + x * span, cross, True),
-        (core * half + cross, span - cross, False),
-    )
+    part = cross // CROSS_PARTS
+    chunks = [
+        (core * half + x * span + n * part, part, True) for n in range(CROSS_PARTS)
+    ] + [(core * half + cross, span - cross, False)]
     cross_other = core * half + (1 - x) * span
     rows = weights.shape[1] // shards
 
@@ -414,49 +415,53 @@
     for store in stores:
         store.start()
 
-    crossed, paired = [], []
+    crossed, paired = [[] for _ in range(shards)], []
+    last = len(chunks) - 1
 
     def arrived(n, slot, owner):
         begin, count, crosses = chunks[n]
         if crosses:
-            copy = pass_on(begin, count, owner, x_send.at[slot], x_recv.at[slot], across)
-            crossed.append((slot, owner, copy))
-        paired.append(
-            pass_on(begin, count, owner, core_send.at[n, slot], core_recv.at[n, slot], sibling)
-        )
-
-    def from_across():
-        slot, owner, copy = crossed.pop(0)
-        copy.wait_recv()
+            copy = pass_on(begin, count, owner, x_send.at[n, slot], x_recv.at[n, slot], across)
+            crossed[slot].append(copy)
+        if n == last:
+            paired.append(
+                pass_on(first, span, owner, core_send.at[0, slot], core_recv.at[0, slot], sibling)
+            )
+
+    def from_across(slot, owner):
+        for copy in crossed[slot]:
+            copy.wait_recv()
         paired.append(
             pass_on(
-                cross_other, cross, owner,
-                core_send.at[len(chunks), slot], core_recv.at[len(chunks), slot], sibling,
-            )
-        )
+                cross_other, cross, owner, core_send.at[1, slot], core_recv.at[1, slot], sibling
+            )
+        )
+
+    def owner_at(d, side):
+        return lax.rem(z + depth - d, depth) * 2 + (y if side == 0 else 1 - y)
+
+    def turned_in(n):
+        for d in range(1, depth):
+            turned[n][d].wait_recv()
+            arrived(n, depth + d, owner_at(d, 1))
 
     for n, (begin, count, _) in enumerate(chunks):
         turned[n][0].wait_recv()
-        arrived(n, depth, z * 2 + 1 - y)
+        arrived(n, depth, owner_at(0, 1))
         for d in range(1, depth):
             along[n][d].wait_recv()
-            owner = lax.rem(z + depth - d, depth) * 2 + y
             turned[n][d] = pass_on(
-                begin, count, owner, y_send.at[n, d], y_recv.at[n, d], beside
-            )
-            arrived(n, d, owner)
-        if n == 0:
-            continue
-        for d in range(1, depth):
-            turned[n - 1][d].wait_recv()
-            arrived(n - 1, depth + d, lax.rem(z + depth - d, depth) * 2 + 1 - y)
-    for _ in range(depth):
-        from_across()
+                begin, count, owner_at(d, 0), y_send.at[n, d], y_recv.at[n, d], beside
+            )
+            arrived(n, d, owner_at(d, 0))
+        if n > 0:
+            turned_in(n - 1)
+    from_across(depth, owner_at(0, 1))
     for d in range(1, depth):
-        turned[-1][d].wait_recv()
-        arrived(len(chunks) - 1, depth + d, lax.rem(z + depth - d, depth) * 2 + 1 - y)
-    while crossed:
-        from_across()
+        from_across(d, owner_at(d, 0))
+    turned_in(last)
+    for d in range(1, depth):
+        from_across(depth + d, owner_at(d, 1))
     for copy in paired:
         copy.wait_recv()
     for copy in started:
@@ -508,7 +513,7 @@
     states = [a.reshape(experts, reps, 8, channels) for a in args[13:16]]
     state = (experts, reps, 8, channels)
     norm_limit = math.sqrt(experts * parts * channels * channels)
-    chunk_total = 2
+    chunk_total = CROSS_PARTS + 1
 
     def held(array):
         return pltpu.VMEM(array.shape, array.dtype)
@@ -549,8 +554,8 @@
             *pairs(devices),
             *pairs(chunk_total, depth),
             *pairs(chunk_total, depth),
-            *pairs(shards),
-            *pairs(chunk_total + 1, shards),
+            *pairs(CROSS_PARTS, shards),
+            *pairs(2, shards),
         ],
         compiler_params=pltpu.CompilerParams(
             collective_id=0, has_side_effects=True, vmem_limit_bytes=60 * MIB

time: 49.2 us -> 49.3 us (level)
  no operation moved by 1% of the time
where the time goes in v4:
time: 49.3 us; the launch traced here: 49.1 us
  Pallas kernels  48.5 us (98%)
  between operations  0.65 us (1%)
    pallas_call x1, Pallas kernels, kernel_local(): pl.pallas_call(functools.partial(whole_kernel, shards, reps, norm_limit),...  44.6 us
    pallas_call x1, Pallas kernels, kernel_local(): pl.pallas_call(finish_kernel, out_shape=outs, in_specs=[anywhere] * 4, ou...  3.86 us

profile of v4, /device:TPU:1, one launch (start us, length us, event | category | flops | bytes accessed | tf_op | source)
XLA Modules:
  0.0 49.1 jit_solution(6151114344317173117)
XLA Ops:
  0.6 44.6 %whole.1 = (f32[32,4,8,128]{3,2,1,0:T(8,128)}, f32[32,4,8,128]{3,2,1,0:T(8,128)}, f32[32,4,8,128]{3,2,1,0:T(8,128)}, bf16[32,256,128]{2,1,0:T(8,128)(2,1)}) custom-call(bf16[8,128,256]{2,1,0:T(8,128)(2,1)} %feat_in.1, bf16[8,128,256]{2,1,0:T(8,128)(2,1)} %cot_in.1, f32[8,1536]{1,0:T(8,128)} %length_in.1, s32[8]{0:T(128)} %atoms_in.1, s32[8]{0:T(128)} %edges_in.1, ...), custom_call_target="tpu_custom_call" | custom-call | tf_op jit(solution)/shard_map/whole/pallas_call | solution.py:526
  45.3 3.9 %finish.1 = (f32[32,4,8,128]{3,2,1,0:T(8,128)}, f32[32,4,8,128]{3,2,1,0:T(8,128)}, f32[32,4,8,128]{3,2,1,0:T(8,128)}, bf16[32,256,128]{2,1,0:T(8,128)(2,1)}) custom-call(f32[32,4,8,128]{3,2,1,0:T(8,128)} %get-tuple-element.12.refs_0_, f32[32,4,8,128]{3,2,1,0:T(8,128)} %get-tuple-element.13.refs_1_, f32[32,4,8,128]{3,2,1,0:T(8,128)} %get-tuple-element.14.refs_2_, ...), custom_call_target="tpu_custom_call" | custom-call | tf_op jit(solution)/shard_map/finish/pallas_call | solution.py:566

commit v5 on v4

--- a/solution.py
+++ b/solution.py
@@ -261,20 +261,18 @@
         [jnp.where(rows_of[s] == k, 1.0, 0.0) for s in range(systems)] for k in range(tags)
     ]
 
-    def group(i, carry):
-        at = pl.multiple_of(i * 8, 8)
-        terms = [products[s, pl.ds(at, 8), :] for s in range(systems)]
-        sums = []
+    block_rows = reps * 8
+
+    def group(owner):
+        at = pl.multiple_of(owner * block_rows, block_rows)
+        terms = [products[s, pl.ds(at, block_rows), :] for s in range(systems)]
         for k in range(tags):
             total = takes[k][0] * terms[0]
             for s in range(1, systems):
                 total = total + takes[k][s] * terms[s]
-            sums.append(total)
-        owner, r = i // reps, lax.rem(i, reps)
-        pieces[lax.rem(r, 2), r // 2, owner] = jnp.concatenate(sums, axis=0)
-        return carry
-
-    lax.fori_loop(0, devices, group, 0, unroll=2)
+            for r in range(reps):
+                pieces[r % 2, r // 2, owner, 8 * k : 8 * k + 8, :] = total[8 * r : 8 * r + 8, :]
+
     pl.semaphore_wait(barrier, devices - 1)
 
     def send(src, dst, send_sem, recv_sem, to):
@@ -293,6 +291,8 @@
     pair, sided, ahead = {}, {}, []
     for dz, to_z in parts:
         both = pl.ds(pl.multiple_of(to_z * 2, 2), 2)
+        group(to_z * 2)
+        group(to_z * 2 + 1)
         pair[dz] = send(
             pieces.at[1 - core, :, both], pair_in.at[:, both],
             pair_sem.at[0, dz], pair_sem.at[1, dz], sibling,

time: 49.3 us -> 48.6 us (0.986)
  Pallas kernels: 48.5 us -> 47.8 us
    pallas_call x1, Pallas kernels: 44.6 us -> 44 us  [kernel_local(): pl.pallas_call(functools.partial(whole_kernel, shards, reps, norm_limit),...]
where the time goes in v5:
time: 48.6 us; the launch traced here: 48.5 us
  Pallas kernels  47.8 us (98%)
  between operations  0.65 us (1%)
    pallas_call x1, Pallas kernels, kernel_local(): pl.pallas_call(functools.partial(whole_kernel, shards, reps, norm_limit),...  44 us
    pallas_call x1, Pallas kernels, kernel_local(): pl.pallas_call(finish_kernel, out_shape=outs, in_specs=[anywhere] * 4, ou...  3.86 us

profile of v5, /device:TPU:1, one launch (start us, length us, event | category | flops | bytes accessed | tf_op | source)
XLA Modules:
  0.0 48.5 jit_solution(14024428765803878325)
XLA Ops:
  0.6 44.0 %whole.1 = (f32[32,4,8,128]{3,2,1,0:T(8,128)}, f32[32,4,8,128]{3,2,1,0:T(8,128)}, f32[32,4,8,128]{3,2,1,0:T(8,128)}, bf16[32,256,128]{2,1,0:T(8,128)(2,1)}) custom-call(bf16[8,128,256]{2,1,0:T(8,128)(2,1)} %feat_in.1, bf16[8,128,256]{2,1,0:T(8,128)(2,1)} %cot_in.1, f32[8,1536]{1,0:T(8,128)} %length_in.1, s32[8]{0:T(128)} %atoms_in.1, s32[8]{0:T(128)} %edges_in.1, ...), custom_call_target="tpu_custom_call" | custom-call | tf_op jit(solution)/shard_map/whole/pallas_call | solution.py:526
  44.6 3.9 %finish.1 = (f32[32,4,8,128]{3,2,1,0:T(8,128)}, f32[32,4,8,128]{3,2,1,0:T(8,128)}, f32[32,4,8,128]{3,2,1,0:T(8,128)}, bf16[32,256,128]{2,1,0:T(8,128)(2,1)}) custom-call(f32[32,4,8,128]{3,2,1,0:T(8,128)} %get-tuple-element.12.refs_0_, f32[32,4,8,128]{3,2,1,0:T(8,128)} %get-tuple-element.13.refs_1_, f32[32,4,8,128]{3,2,1,0:T(8,128)} %get-tuple-element.14.refs_2_, ...), custom_call_target="tpu_custom_call" | custom-call | tf_op jit(solution)/shard_map/finish/pallas_call | solution.py:566

commit v6 on v5

--- a/solution.py
+++ b/solution.py
@@ -161,7 +161,7 @@
     channels = width // 2
     lanes = source.shape[1]
 
-    def one_system(s, carry):
+    def selectors(s):
         slot_index = lax.broadcasted_iota(jnp.int32, (1, lanes), 1)
         atom_index = lax.broadcasted_iota(jnp.int32, (slots, lanes), 0)
         count = jnp.full((1, lanes), atoms[s], jnp.int32).astype(jnp.float32)
@@ -169,9 +169,9 @@
         row = weight[pl.ds(s, 1), :] * factor
         left = jnp.where(atom_index == source[pl.ds(s, 1), :], row, 0.0).astype(jnp.bfloat16)
         right = jnp.where(atom_index == target[pl.ds(s, 1), :], 1.0, 0.0).astype(jnp.bfloat16)
-        pairs = lax.dot_general(
-            right, left, (((1,), (1,)), ((), ())), preferred_element_type=jnp.float32
-        )
+        return left, right
+
+    def system_product(s, pairs):
         mixed = split_dot_left(pairs, cot[s])
         real, imag = mixed[:, :channels], mixed[:, channels:]
         block = jnp.concatenate(
@@ -186,12 +186,23 @@
         product = split_dot(stacked, block, ((0,), (0,)))
         products[s, pl.ds(0, channels, stride=2), :] = product[:, :channels]
         products[s, pl.ds(1, channels, stride=2), :] = product[:, channels:]
+
+    def some_systems(i, carry):
+        chosen = [selectors(i * STACKED + n) for n in range(STACKED)]
+        left = jnp.concatenate([c[0] for c in chosen], axis=0)
+        right = jnp.concatenate([c[1] for c in chosen], axis=0)
+        pairs = lax.dot_general(
+            right, left, (((1,), (1,)), ((), ())), preferred_element_type=jnp.float32
+        )
+        for n in range(STACKED):
+            own = slice(n * slots, (n + 1) * slots)
+            system_product(i * STACKED + n, pairs[own, own])
         return carry
 
-    lax.fori_loop(0, systems, one_system, 0, unroll=UNROLL_SYSTEMS)
-
-
-UNROLL_SYSTEMS = 4
+    lax.fori_loop(0, systems // STACKED, some_systems, 0, unroll=2)
+
+
+STACKED = 2
 CROSS_PARTS = 2
 
 
@@ -599,7 +610,8 @@
 
     def local(*args):
         params = args[13]
-        if reps == 4 and shards % 2 == 0 and params.shape[1] * params.shape[2] == 8 * reps:
+        even = shards % 2 == 0 and args[2].shape[0] % STACKED == 0
+        if reps == 4 and even and params.shape[1] * params.shape[2] == 8 * reps:
             return kernel_local(shards, reps, *args)
         return plain_local(*args)
 

time: 48.6 us -> 48.7 us (level)
  no operation moved by 1% of the time
where the time goes in v6:
time: 48.7 us; the launch traced here: 48.5 us
  Pallas kernels  47.9 us (98%)
  between operations  0.65 us (1%)
    pallas_call x1, Pallas kernels, kernel_local(): pl.pallas_call(functools.partial(whole_kernel, shards, reps, norm_limit),...  44 us
    pallas_call x1, Pallas kernels, kernel_local(): pl.pallas_call(finish_kernel, out_shape=outs, in_specs=[anywhere] * 4, ou...  3.86 us

profile of v6, /device:TPU:1, one launch (start us, length us, event | category | flops | bytes accessed | tf_op | source)
XLA Modules:
  0.0 48.5 jit_solution(3047128147378771813)
XLA Ops:
  0.6 44.0 %whole.1 = (f32[32,4,8,128]{3,2,1,0:T(8,128)}, f32[32,4,8,128]{3,2,1,0:T(8,128)}, f32[32,4,8,128]{3,2,1,0:T(8,128)}, bf16[32,256,128]{2,1,0:T(8,128)(2,1)}) custom-call(bf16[8,128,256]{2,1,0:T(8,128)(2,1)} %feat_in.1, bf16[8,128,256]{2,1,0:T(8,128)(2,1)} %cot_in.1, f32[8,1536]{1,0:T(8,128)} %length_in.1, s32[8]{0:T(128)} %atoms_in.1, s32[8]{0:T(128)} %edges_in.1, ...), custom_call_target="tpu_custom_call" | custom-call | tf_op jit(solution)/shard_map/whole/pallas_call | solution.py:537
  44.7 3.9 %finish.1 = (f32[32,4,8,128]{3,2,1,0:T(8,128)}, f32[32,4,8,128]{3,2,1,0:T(8,128)}, f32[32,4,8,128]{3,2,1,0:T(8,128)}, bf16[32,256,128]{2,1,0:T(8,128)(2,1)}) custom-call(f32[32,4,8,128]{3,2,1,0:T(8,128)} %get-tuple-element.12.refs_0_, f32[32,4,8,128]{3,2,1,0:T(8,128)} %get-tuple-element.13.refs_1_, f32[32,4,8,128]{3,2,1,0:T(8,128)} %get-tuple-element.14.refs_2_, ...), custom_call_target="tpu_custom_call" | custom-call | tf_op jit(solution)/shard_map/finish/pallas_call | solution.py:577
